TPU v7x, 32 devices: a whole 2x2x4 slice. The times are simulated.
32 devices in a mesh: groups: 1, tensor: 16 (over z, y, core), replica: 2 (over x).
Axes of the slice: x: 2, y: 2, z: 4, core: 2. Of those that a mesh axis runs over, the one named last changes fastest.
Arguments:
- q_latent: bfloat16 [256, 1536], P(('groups', 'tensor', 'replica')), may hold values from -6 to 6
- q_gain: float32 [1536], replicated, may hold values from 0.25 to 1.75
- q_up: bfloat16 [1536, 12288], P(None, 'tensor'), may hold values from -0.15625 to 0.15625
- w_uk: bfloat16 [64, 128, 512], P('tensor'), may hold values from -0.5 to 0.5
- w_uv: bfloat16 [64, 512, 128], P('tensor'), may hold values from -1 to 1
- w_o: bfloat16 [8192, 7168], P('tensor', 'replica'), may hold values from -0.0625 to 0.0625
- new_kv: bfloat16 [256, 576], P(('groups', 'tensor', 'replica')), may hold values from -6 to 6
- latent_cache: bfloat16 [64, 1024, 576], P(('groups', 'tensor', 'replica')), may hold values from -64 to 64
- cache_len: int32 [64], P(('groups', 'tensor', 'replica')), may hold values from 128 to 1024, as said below
- draft_count: int32 [64], P(('groups', 'tensor', 'replica')), may hold values from 1 to 4, as said below
Outputs:
- attn_out: bfloat16 [256, 7168], P(('groups', 'tensor', 'replica'))
Inputs may be any that keep to these rules, and one draw needn't show every extreme that they name: `cache_len`: some request of every draw uses all 1024 slots. The first draft_count rows of a request are in use; some request of every draw uses all 4.
All inputs are finite; a program needn't handle non-finite values.
Results may differ from a plain program's by a relative error of at most 0.024.
The roundings to bfloat16 on the way count: a program that leaves them out, or rounds other values in their place, can miss the bound.
Values may be sent and summed in bfloat16 or wider, within the bound.
A program may use at most 64 MiB of HBM per device.

v0:
```python
import jax
import jax.numpy as jnp
from jax import lax
from jax.sharding import PartitionSpec as P

LATENT = 512
ROPE = 64
NOPE = 128
VDIM = 128
DRAFT = 4
REQ_DEV = 2


rms_eps = 1e-06
rope_base = 50000.0


def normalize(rows_in, gain_row):
    values_f = rows_in.astype(jnp.float32)
    scaled = values_f * lax.rsqrt(jnp.mean(values_f * values_f, axis=-1, keepdims=True) + rms_eps)
    return (scaled * gain_row).astype(jnp.bfloat16)


def rotate(rope_part, positions):
    half_width = rope_part.shape[-1] // 2
    frequency = rope_base ** (
        -(jnp.arange(half_width).astype(jnp.float32) * 2.0 / rope_part.shape[-1])
    )
    angles = positions[:, None, None] * frequency
    cosine = jnp.cos(angles)
    sine = jnp.sin(angles)
    widened = rope_part.astype(jnp.float32)
    first_half = widened[..., :half_width]
    second_half = widened[..., half_width:]
    turned = jnp.concatenate(
        [first_half * cosine - second_half * sine, second_half * cosine + first_half * sine],
        axis=-1,
    )
    return turned.astype(jnp.bfloat16)


def attend(query_rows, new_rows, cache_rows, length, draft_total):
    queries = query_rows.reshape(-1, query_rows.shape[-1])
    contract = (((1,), (1,)), ((), ()))
    score_scale = (NOPE + ROPE) ** (-0.5)
    cache_scores = (
        lax.dot_general(queries, cache_rows, contract, preferred_element_type=jnp.float32)
        * score_scale
    )
    new_scores = (
        lax.dot_general(queries, new_rows, contract, preferred_element_type=jnp.float32)
        * score_scale
    )
    row_draft = jnp.arange(queries.shape[0]) // query_rows.shape[1]
    cache_seen = jnp.arange(cache_rows.shape[0]) < length
    new_seen = jnp.arange(new_rows.shape[0])[None, :] <= row_draft[:, None]
    cache_scores = jnp.where(cache_seen[None, :], cache_scores, -jnp.inf)
    new_scores = jnp.where(new_seen, new_scores, -jnp.inf)
    row_peak = jnp.maximum(jnp.max(cache_scores, axis=1), jnp.max(new_scores, axis=1))[:, None]
    cache_exp = jnp.exp(cache_scores - row_peak)
    new_exp = jnp.exp(new_scores - row_peak)
    denominator = jnp.sum(cache_exp, axis=1, keepdims=True) + jnp.sum(
        new_exp, axis=1, keepdims=True
    )
    cache_weights = (cache_exp / denominator).astype(jnp.bfloat16)
    new_weights = (new_exp / denominator).astype(jnp.bfloat16)
    latent_mix = jnp.dot(cache_weights, cache_rows[:, :LATENT], preferred_element_type=jnp.float32)
    latent_mix = latent_mix + jnp.dot(
        new_weights, new_rows[:, :LATENT], preferred_element_type=jnp.float32
    )
    latent_mix = jnp.where((row_draft < draft_total)[:, None], latent_mix, 0.0).astype(jnp.bfloat16)
    return latent_mix.reshape(query_rows.shape[0], query_rows.shape[1], LATENT)


def shards(q_latent, q_gain, q_up, w_uk, w_uv, w_o, new_kv, latent_cache, cache_len, draft_count):
    rows_dev = q_latent.shape[0]
    owners = lax.axis_size("tensor")
    heads_dev = w_uk.shape[0]
    head_count = heads_dev * owners
    normed = normalize(q_latent, q_gain)
    query_full = jnp.dot(
        lax.all_gather(normed, "tensor", axis=0, tiled=True),
        q_up,
        preferred_element_type=jnp.float32,
    ).astype(jnp.bfloat16)
    query_full = query_full.reshape(owners, rows_dev, heads_dev, NOPE + ROPE)
    absorbed = jnp.einsum(
        "pihn,hnl->iphl", query_full[..., :NOPE], w_uk, preferred_element_type=jnp.float32
    ).astype(jnp.bfloat16)
    rope_part = jnp.swapaxes(query_full[..., NOPE:], 0, 1)
    packed_queries = jnp.concatenate([absorbed, rope_part], axis=-1).reshape(
        rows_dev, owners, heads_dev * (LATENT + ROPE)
    )
    arrived = lax.all_to_all(packed_queries, "tensor", split_axis=1, concat_axis=1, tiled=True)
    arrived = arrived.reshape(rows_dev, head_count, LATENT + ROPE)
    row_length = jnp.broadcast_to(cache_len[:, None], (REQ_DEV, DRAFT)).reshape(-1)
    positions = (row_length + jnp.arange(rows_dev) % DRAFT).astype(jnp.float32)
    rotated = rotate(arrived[..., LATENT:], positions)
    query = jnp.concatenate([arrived[..., :LATENT], rotated], axis=-1)
    latent_out = jax.vmap(attend)(
        query.reshape(REQ_DEV, DRAFT, head_count, LATENT + ROPE),
        new_kv.reshape(REQ_DEV, DRAFT, LATENT + ROPE),
        latent_cache,
        cache_len,
        draft_count,
    )
    latent_out = latent_out.reshape(rows_dev, owners, heads_dev * LATENT)
    returned = lax.all_to_all(latent_out, "tensor", split_axis=1, concat_axis=1, tiled=True)
    returned = returned.reshape(rows_dev, owners, heads_dev, LATENT)
    head_values = jnp.einsum(
        "ithl,hlv->tihv", returned, w_uv, preferred_element_type=jnp.float32
    ).astype(jnp.bfloat16)
    head_values = head_values.reshape(owners * rows_dev, heads_dev * VDIM)
    replicas = lax.axis_size("replica")
    spread = lax.all_gather(head_values, "replica", axis=0, tiled=True)
    spread = spread.reshape(replicas, owners, rows_dev, heads_dev * VDIM)
    block_rows = replicas * rows_dev
    product = jnp.einsum("rtiv,vc->tric", spread, w_o, preferred_element_type=jnp.float32)
    shares = lax.psum_scatter(
        product.reshape(block_rows * lax.axis_size("tensor"), w_o.shape[1]).astype(jnp.bfloat16),
        "tensor",
        scatter_dimension=0,
        tiled=True,
    ).astype(jnp.float32)
    shares = shares.astype(jnp.bfloat16).reshape(replicas, rows_dev, w_o.shape[1])
    placed = lax.all_to_all(shares, "replica", split_axis=0, concat_axis=2, tiled=True)
    return placed.reshape(rows_dev, replicas * w_o.shape[1])


def solution(mesh):
    return jax.shard_map(
        shards,
        mesh=mesh,
        in_specs=(
            P(("groups", "tensor", "replica"), None),
            P(),
            P(None, "tensor"),
            P("tensor", None, None),
            P("tensor", None, None),
            P("tensor", "replica"),
            P(("groups", "tensor", "replica"), None),
            P(("groups", "tensor", "replica"), None, None),
            P(("groups", "tensor", "replica")),
            P(("groups", "tensor", "replica")),
        ),
        out_specs=P(("groups", "tensor", "replica"), None),
        check_vma=False,
    )
```

profile of v0, /device:TPU:0, one launch (start us, length us, event | category | flops | bytes accessed | tf_op | source)
XLA Modules:
  0.0 170.3 jit_solution(1543536647572965304)
XLA Ops:
  6.5 1.0 fusion.27
  7.6 0.8 fusion.29
  8.4 24.1 %all_gather.6 = bf16[128,1536]{1,0:T(8,128)(2,1)S(1)} all-gather(bf16[8,1536]{1,0:T(8,128)(2,1)S(1)} %fusion.29), channel_id=1, replica_groups=mesh['groups'=1,'tensor'=16,'replica'=2] {'tensor'}, dimensions={0}, use_global_device_ids=true | all-gather | bytes 417792 | tf_op jit(solution)/shard_map/all_gather | solution.py:82
  32.5 0.5 convolution_convert_fusion.2
  34.0 0.5 copy.53
  34.5 1.3 reshape.221
  35.8 3.6 %all-to-all-start = ((bf16[8,16,2304]{2,0,1:T(8,128)(2,1)}), bf16[8,16,2304]{2,0,1:T(8,128)(2,1)S(1)}, u32[]{:S(2)}, u32[]{:S(2)}) async-start(bf16[8,16,2304]{2,0,1:T(8,128)(2,1)} %reshape.221), calls=%async_computation | async-start | bytes 1179648 | tf_op jit(solution)/shard_map/all_to_all | solution.py:94
  39.9 15.0 %all-to-all-done = bf16[8,16,2304]{2,0,1:T(8,128)(2,1)S(1)} async-done(((bf16[8,16,2304]{2,0,1:T(8,128)(2,1)}), bf16[8,16,2304]{2,0,1:T(8,128)(2,1)S(1)}, u32[]{:S(2)}, u32[]{:S(2)}) %all-to-all-start) | async-done | bytes 589856 | tf_op jit(solution)/shard_map/all_to_all | solution.py:94
  54.9 0.9 copy.39
  55.8 1.9 %reshape.209 = bf16[8,64,576]{2,1,0:T(8,128)(2,1)S(1)} reshape(bf16[8,16,2304]{2,1,0:T(8,128)(2,1)} %copy.39) | data formatting | bytes 1179648 | tf_op jit(solution)/shard_map/reshape | solution.py:95
  58.4 1.0 copy-done.5
  59.4 1.1 fusion.4
  60.5 0.6 fusion.5
  61.1 0.4 fusion.30
  61.4 1.1 fusion.12
  63.2 18.6 %all_to_all.25 = bf16[8,16,2048]{2,0,1:T(8,128)(2,1)S(1)} all-to-all(bf16[8,16,2048]{2,0,1:T(8,128)(2,1)S(1)} %copy.43), channel_id=1, replica_groups=mesh['groups'=1,'tensor'=16,'replica'=2] {'tensor'}, dimensions={1} | all-to-all | bytes 1048576 | tf_op jit(solution)/shard_map/all_to_all | solution.py:108
  81.8 0.4 reshape.222
  82.2 1.7 %fusion.16 = bf16[16,8,4,128]{3,0,1,2:T(8,128)(2,1)S(1)} fusion(bf16[4,512,128]{2,1,0:T(8,128)(2,1)} %param.14, bf16[8,16,4,512]{3,2,0,1:T(4,128)(2,1)S(1)} %reshape.222), kind=kOutput, calls=%fused_computation.17 | convolution fusion | flops 67174400 | bytes 1179648 | tf_op jit(solution)/shard_map/ithl,hlv->tihv/dot_general | solution.py:110
  84.0 6.1 %all_gather.7 = bf16[256,512]{1,0:T(8,128)(2,1)S(1)} all-gather(bf16[128,512]{1,0:T(8,128)(2,1)S(1)} %bitcast.51), channel_id=1, replica_groups=mesh['groups'=1,'tensor'=16,'replica'=2] {'replica'}, dimensions={0}, use_global_device_ids=true | all-gather | bytes 393216 | tf_op jit(solution)/shard_map/all_gather | solution.py:115
  90.1 3.2 %fusion = bf16[16,2,8,3584]{3,2,0,1:T(8,128)(2,1)S(1)} fusion(bf16[2,16,8,512]{3,2,1,0:T(8,128)(2,1)S(1)} %bitcast.53, bf16[512,3584]{1,0:T(8,128)(2,1)} %param.15), kind=kOutput, calls=%fused_computation.1 | convolution fusion | flops 940441600 | bytes 5767168 | tf_op jit(solution)/shard_map/rtiv,vc->tric/dot_general | solution.py:118
  93.2 1.4 copy.47
  94.7 60.4 %reduce-scatter.2.cloned.1.call-done = bf16[16,3584]{1,0:T(8,128)(2,1)} async-done(((bf16[256,3584]{1,0:T(8,128)(2,1)}), bf16[16,3584]{1,0:T(8,128)(2,1)}) %reduce-scatter.2.cloned.1.call-update) | async-done | bytes 114704 | tf_op jit(solution)/shard_map/reduce_scatter | solution.py:119
  155.1 7.7 %all_to_all.26 = bf16[2,8,3584]{2,1,0:T(8,128)(2,1)S(1)} all-to-all(bf16[2,8,3584]{2,1,0:T(8,128)(2,1)} %bitcast.54), channel_id=1, replica_groups=mesh['groups'=1,'tensor'=16,'replica'=2] {'replica'}, dimensions={0} | all-to-all | bytes 229376 | tf_op jit(solution)/shard_map/all_to_all | solution.py:126
  162.8 0.6 copy.69
  (41 shorter events, 2.7 us)
Async XLA Ops:
  6.5 26.0 %copy-start = (bf16[1536,768]{1,0:T(8,128)(2,1)S(1)}, bf16[1536,768]{1,0:T(8,128)(2,1)}, u32[]{:S(2)}) copy-start(bf16[1536,768]{1,0:T(8,128)(2,1)} %param.12) | copy-start | bytes 7077892
  32.5 1.0 copy-start.1
  33.9 5.5 %copy-start.4 = (s32[2]{0:T(128)S(1)}, s32[2]{0:T(128)}, u32[]{:S(2)}) copy-start(s32[2]{0:T(128)} %param.18) | copy-start | bytes 28
  33.9 5.7 %copy-start.2 = (bf16[8,576]{1,0:T(8,128)(2,1)S(1)}, bf16[8,576]{1,0:T(8,128)(2,1)}, u32[]{:S(2)}) copy-start(bf16[8,576]{1,0:T(8,128)(2,1)} %param.16) | copy-start | bytes 27652
  34.0 5.7 %copy-start.3 = (s32[2]{0:T(128)S(1)}, s32[2]{0:T(128)}, u32[]{:S(2)}) copy-start(s32[2]{0:T(128)} %param.19) | copy-start | bytes 28
  35.8 19.1 %all-to-all-start = ((bf16[8,16,2304]{2,0,1:T(8,128)(2,1)}), bf16[8,16,2304]{2,0,1:T(8,128)(2,1)S(1)}, u32[]{:S(2)}, u32[]{:S(2)}) async-start(bf16[8,16,2304]{2,0,1:T(8,128)(2,1)} %reshape.221), calls=%async_computation | async-start | bytes 1179648 | tf_op jit(solution)/shard_map/all_to_all | solution.py:94
  39.4 115.7 %reduce-scatter.2.cloned.1.call-start = ((), (), s32[]{:S(2)}) async-start(), calls=%async_computation.4 | async-start | bytes 1949696 | tf_op jit(solution)/shard_map/reduce_scatter | solution.py:119
  57.7 1.7 copy-start.5
Sparse Core Ops, SparseCore 0:
  94.8 60.2 reduce-scatter.1
where the time goes:
time: 171 us; the launch traced here: 170 us
  waiting for transfers between devices  75.4 us (44%)
  blocking collectives  56.6 us (33%)
  between operations  13.7 us (8%)
  local copies, waits for them, and re-layouts  9.49 us (6%)
  matrix products  8.49 us (5%)
  starting transfers between devices  3.62 us (2%)
  other arithmetic  3.07 us (2%)
    reduce_scatter x1, waiting for transfers between devices, shards(): lax.psum_scatter(product.reshape(block_rows * lax.axis_size('tensor'), w_...  60.4 us
    all_gather x1, blocking collectives, shards(): lax.all_gather(normed, 'tensor', axis=0, tiled=True)  24.1 us
    all_to_all x1, blocking collectives, shards(): lax.all_to_all(latent_out, 'tensor', split_axis=1, concat_axis=1, tiled=T...  18.6 us
    all_to_all x1, waiting for transfers between devices, shards(): lax.all_to_all(packed_queries, 'tensor', split_axis=1, concat_axis=1, til...  15 us
    all_to_all x1, blocking collectives, shards(): lax.all_to_all(shares, 'replica', split_axis=0, concat_axis=2, tiled=True)  7.73 us
    all_gather x1, blocking collectives, shards(): spread = lax.all_gather(head_values, 'replica', axis=0, tiled=True)  6.09 us
    all_to_all x1, starting transfers between devices, shards(): lax.all_to_all(packed_queries, 'tensor', split_axis=1, concat_axis=1, til...  3.58 us
  transfers between devices with their start and end apart: 2, of which 2 were waited for; matrix products, arithmetic and copies ran while one was open for 0% of the time, Pallas kernels for 0%

commit v1 on v0

--- a/solution.py
+++ b/solution.py
@@ -1,6 +1,10 @@
+import functools
+
 import jax
 import jax.numpy as jnp
 from jax import lax
+from jax.experimental import pallas as pl
+from jax.experimental.pallas import tpu as pltpu
 from jax.sharding import PartitionSpec as P
 
 LATENT = 512
@@ -9,6 +13,7 @@
 VDIM = 128
 DRAFT = 4
 REQ_DEV = 2
+MESH = pl.DeviceIdType.MESH
 
 
 rms_eps = 1e-06
@@ -70,6 +75,220 @@
     )
     latent_mix = jnp.where((row_draft < draft_total)[:, None], latent_mix, 0.0).astype(jnp.bfloat16)
     return latent_mix.reshape(query_rows.shape[0], query_rows.shape[1], LATENT)
+
+
+def split_axis(count):
+    near = 2 if count % 2 == 0 else 1
+    side = 2 if (count // near) % 2 == 0 else 1
+    return near, side, count // near // side
+
+
+def column_chunks(width):
+    for parts in (4, 3, 2):
+        if width % (parts * 128) == 0:
+            return parts
+    return 1
+
+
+def meet(partners):
+    barrier = pltpu.get_barrier_semaphore()
+    for partner in partners:
+        pl.semaphore_signal(barrier, inc=1, device_id=partner, device_id_type=MESH)
+    pl.semaphore_wait(barrier, len(partners))
+
+
+def place():
+    group = lax.axis_index("groups")
+    me = lax.axis_index("tensor")
+    copy = lax.axis_index("replica")
+    return group, me, copy
+
+
+def project(sizes, hv_ref, wo_ref, out_ref, spread, wo, sent1, got1, sent2, got2, kept2, sent3,
+            got3, kept3, sentx, gotx, wo_sem, hs, hr, s1, r1, s2, r2, s3, r3, sx, rx):
+    tensors, copies, rows_dev = sizes
+    near, side, far = split_axis(tensors)
+    parts = column_chunks(wo_ref.shape[1])
+    width = wo_ref.shape[1] // parts
+    group, me, copy = place()
+    c = lax.rem(me, near)
+    y = lax.rem(me // near, side)
+    z = me // (near * side)
+
+    def at(z_to, y_to, c_to):
+        return (group, (z_to * side + y_to) * near + c_to, copy)
+
+    def twin(step):
+        return lax.rem(copy + step, copies)
+
+    loads = [
+        pltpu.make_async_copy(
+            wo_ref.at[:, pl.ds(k * width, width)], wo.at[k], wo_sem.at[k]
+        )
+        for k in range(parts)
+    ]
+    for load in loads:
+        load.start()
+    near_peers = [at(z, y, lax.rem(c + d, near)) for d in range(1, near)]
+    side_peers = [at(z, lax.rem(y + d, side), c) for d in range(1, side)]
+    far_peers = [at(lax.rem(z + d, far), y, c) for d in range(1, far)]
+    twin_peers = [(group, me, twin(d)) for d in range(1, copies)]
+    meet(near_peers + side_peers + far_peers + twin_peers)
+
+    def send(src, dst, send_sem, recv_sem, peer):
+        push = pltpu.make_async_remote_copy(
+            src_ref=src, dst_ref=dst, send_sem=send_sem, recv_sem=recv_sem,
+            device_id=peer, device_id_type=MESH,
+        )
+        push.start()
+        return push
+
+    spread_out = [
+        send(hv_ref, spread.at[d - 1], hs.at[d - 1], hr.at[d - 1], twin_peers[d - 1])
+        for d in range(1, copies)
+    ]
+
+    pushes1, pushes2, pushes3, pushesx = {}, {}, {}, {}
+
+    def multiply(k):
+        loads[k].wait()
+        weights = wo[k]
+        own = jnp.dot(hv_ref[...], weights, preferred_element_type=jnp.float32)
+        if k == 0:
+            for push in spread_out:
+                push.wait_recv()
+        others = [
+            jnp.dot(spread[d], weights, preferred_element_type=jnp.float32)
+            for d in range(copies - 1)
+        ]
+        by_step = [own] + others
+        if copies == 2:
+            swap = copy == 1
+            ordered = [jnp.where(swap, by_step[1], by_step[0]), jnp.where(swap, by_step[0], by_step[1])]
+        else:
+            ordered = []
+            for slot in range(copies):
+                chosen = by_step[0]
+                for d in range(1, copies):
+                    chosen = jnp.where(lax.rem(copy - d + copies, copies) == slot, by_step[d], chosen)
+                ordered.append(chosen)
+        for t in range(tensors):
+            block = jnp.concatenate([o[t * rows_dev : (t + 1) * rows_dev] for o in ordered], axis=0)
+            ct, yt, zt = t % near, (t // near) % side, t // (near * side)
+            sent1[k, ct, yt, zt] = block.astype(jnp.bfloat16)
+        pushes1[k] = [
+            send(sent1.at[k, lax.rem(c + d, near)], got1.at[k, d - 1],
+                 s1.at[k, d - 1], r1.at[k, d - 1], near_peers[d - 1])
+            for d in range(1, near)
+        ]
+
+    def sum_near(k):
+        for push in pushes1[k]:
+            push.wait_recv()
+        for d in range(side):
+            to = lax.rem(y + d, side)
+            total = sent1[k, c, to].astype(jnp.float32)
+            for e in range(near - 1):
+                total = total + got1[k, e, to].astype(jnp.float32)
+            if d == 0:
+                kept2[k] = total
+            else:
+                sent2[k, d - 1] = total.astype(jnp.bfloat16)
+        pushes2[k] = [
+            send(sent2.at[k, d - 1], got2.at[k, d - 1], s2.at[k, d - 1], r2.at[k, d - 1],
+                 side_peers[d - 1])
+            for d in range(1, side)
+        ]
+
+    def sum_side(k):
+        for push in pushes2[k]:
+            push.wait_recv()
+        pushes3[k] = []
+        for d in list(range(1, far)) + [0]:
+            to = lax.rem(z + d, far)
+            total = kept2[k, to]
+            for e in range(side - 1):
+                total = total + got2[k, e, to].astype(jnp.float32)
+            if d == 0:
+                kept3[k] = total
+            else:
+                sent3[k, d - 1] = total.astype(jnp.bfloat16)
+                pushes3[k].append(
+                    send(sent3.at[k, d - 1], got3.at[k, d - 1], s3.at[k, d - 1],
+                         r3.at[k, d - 1], far_peers[d - 1])
+                )
+
+    def sum_far(k):
+        for push in pushes3[k]:
+            push.wait_recv()
+        total = kept3[k]
+        for e in range(far - 1):
+            total = total + got3[k, e].astype(jnp.float32)
+        for r in range(copies):
+            sentx[k, r] = total[r * rows_dev : (r + 1) * rows_dev]
+        pushesx[k] = [
+            send(sentx.at[k, twin(d)], gotx.at[k, d - 1], sx.at[k, d - 1], rx.at[k, d - 1],
+                 twin_peers[d - 1])
+            for d in range(1, copies)
+        ]
+        out_ref[copy, :, k * width : (k + 1) * width] = sentx[k, copy]
+
+    def finish(k):
+        for d in range(1, copies):
+            pushesx[k][d - 1].wait_recv()
+            origin = lax.rem(copy - d + copies, copies)
+            out_ref[origin, :, k * width : (k + 1) * width] = gotx[k, d - 1]
+
+    stages = (multiply, sum_near, sum_side, sum_far, finish)
+    for step in range(parts + len(stages) - 1):
+        for depth, stage in enumerate(stages):
+            if 0 <= step - depth < parts:
+                stage(step - depth)
+    for push in spread_out:
+        push.wait_send()
+    for table in (pushes1, pushes2, pushes3, pushesx):
+        for k in range(parts):
+            for push in table[k]:
+                push.wait_send()
+
+
+def project_call(head_values, w_o, tensors, copies, rows_dev):
+    near, side, far = split_axis(tensors)
+    parts = column_chunks(w_o.shape[1])
+    width = w_o.shape[1] // parts
+    block = copies * rows_dev
+    bf16, f32 = jnp.bfloat16, jnp.float32
+    dma = pltpu.SemaphoreType.DMA
+    n1, n2, n3, nx = (max(v - 1, 1) for v in (near, side, far, copies))
+    return pl.pallas_call(
+        functools.partial(project, (tensors, copies, rows_dev)),
+        out_shape=jax.ShapeDtypeStruct((copies, rows_dev, w_o.shape[1]), f32),
+        in_specs=[pl.BlockSpec(memory_space=pltpu.VMEM), pl.BlockSpec(memory_space=pl.ANY)],
+        out_specs=pl.BlockSpec(memory_space=pltpu.VMEM),
+        scratch_shapes=[
+            pltpu.VMEM((nx,) + head_values.shape, bf16),
+            pltpu.VMEM((parts, w_o.shape[0], width), bf16),
+            pltpu.VMEM((parts, near, side, far, block, width), bf16),
+            pltpu.VMEM((parts, n1, side, far, block, width), bf16),
+            pltpu.VMEM((parts, n2, far, block, width), bf16),
+            pltpu.VMEM((parts, n2, far, block, width), bf16),
+            pltpu.VMEM((parts, far, block, width), f32),
+            pltpu.VMEM((parts, n3, block, width), bf16),
+            pltpu.VMEM((parts, n3, block, width), bf16),
+            pltpu.VMEM((parts, block, width), f32),
+            pltpu.VMEM((parts, copies, rows_dev, width), f32),
+            pltpu.VMEM((parts, nx, rows_dev, width), f32),
+            dma((parts,)),
+            dma((nx,)), dma((nx,)),
+            dma((parts, n1)), dma((parts, n1)),
+            dma((parts, n2)), dma((parts, n2)),
+            dma((parts, n3)), dma((parts, n3)),
+            dma((parts, nx)), dma((parts, nx)),
+        ],
+        compiler_params=pltpu.CompilerParams(
+            collective_id=3, has_side_effects=True, vmem_limit_bytes=48 * 1024 * 1024
+        ),
+    )(head_values, w_o)
 
 
 def shards(q_latent, q_gain, q_up, w_uk, w_uv, w_o, new_kv, latent_cache, cache_len, draft_count):
@@ -112,19 +331,9 @@
     ).astype(jnp.bfloat16)
     head_values = head_values.reshape(owners * rows_dev, heads_dev * VDIM)
     replicas = lax.axis_size("replica")
-    spread = lax.all_gather(head_values, "replica", axis=0, tiled=True)
-    spread = spread.reshape(replicas, owners, rows_dev, heads_dev * VDIM)
-    block_rows = replicas * rows_dev
-    product = jnp.einsum("rtiv,vc->tric", spread, w_o, preferred_element_type=jnp.float32)
-    shares = lax.psum_scatter(
-        product.reshape(block_rows * lax.axis_size("tensor"), w_o.shape[1]).astype(jnp.bfloat16),
-        "tensor",
-        scatter_dimension=0,
-        tiled=True,
-    ).astype(jnp.float32)
-    shares = shares.astype(jnp.bfloat16).reshape(replicas, rows_dev, w_o.shape[1])
-    placed = lax.all_to_all(shares, "replica", split_axis=0, concat_axis=2, tiled=True)
-    return placed.reshape(rows_dev, replicas * w_o.shape[1])
+    placed = project_call(head_values, w_o, owners, replicas, rows_dev)
+    placed = jnp.swapaxes(placed, 0, 1).reshape(rows_dev, replicas * w_o.shape[1])
+    return placed.astype(jnp.bfloat16)
 
 
 def solution(mesh):

time: 171 us -> 110 us (0.64)
  waiting for transfers between devices: 75.4 us -> 15 us
  Pallas kernels: 0 us -> 29.6 us
  blocking collectives: 56.6 us -> 42.8 us
  between operations: 13.7 us -> 0.27 us
  matrix products: 8.49 us -> 5.33 us
    reduce_scatter x1 -> x0, waiting for transfers between devices: 60.4 us -> none  [shards(): lax.psum_scatter(product.reshape(block_rows * lax.axis_size('tensor'), w_...]
    pallas_call x0 -> x1, Pallas kernels: none -> 29.6 us  [project_call(): pl.pallas_call(functools.partial(project, (tensors, copies, rows_dev)), o...]
    all_to_all x1 -> x0, blocking collectives: 7.73 us -> none  [shards(): lax.all_to_all(shares, 'replica', split_axis=0, concat_axis=2, tiled=True)]
    all_gather x1 -> x0, blocking collectives: 6.09 us -> none  [shards(): spread = lax.all_gather(head_values, 'replica', axis=0, tiled=True)]
    dot_general x1 -> x0, matrix products: 3.16 us -> none  [shards(): jnp.einsum('rtiv,vc->tric', spread, w_o, preferred_element_type=jnp.float32)]
  transfers between devices with their start and end apart: 2 -> 1, of which waited for: 2 -> 1; matrix products, arithmetic and copies ran while one was open for 0% -> 0% of each run, Pallas kernels for 0% -> 0%
where the time goes in v1:
time: 110 us
  blocking collectives  42.8 us (39%)
  Pallas kernels  29.6 us (27%)
  waiting for transfers between devices  15 us (14%)
  local copies, waits for them, and re-layouts  9.44 us (9%)
  matrix products  5.33 us (5%)
  other arithmetic  3.73 us (3%)
  starting transfers between devices  3.58 us (3%)
    pallas_call x1, Pallas kernels, project_call(): pl.pallas_call(functools.partial(project, (tensors, copies, rows_dev)), o...  29.6 us
    all_gather x1, blocking collectives, shards(): lax.all_gather(normed, 'tensor', axis=0, tiled=True)  24.1 us
    all_to_all x1, blocking collectives, shards(): lax.all_to_all(latent_out, 'tensor', split_axis=1, concat_axis=1, tiled=T...  18.6 us
    all_to_all x1, waiting for transfers between devices, shards(): lax.all_to_all(packed_queries, 'tensor', split_axis=1, concat_axis=1, til...  15 us
    all_to_all x1, starting transfers between devices, shards(): lax.all_to_all(packed_queries, 'tensor', split_axis=1, concat_axis=1, til...  3.58 us
    unnamed x15, local copies, waits for them, and re-layouts  3.24 us
  transfers between devices with their start and end apart: 1, of which 1 were waited for; matrix products, arithmetic and copies ran while one was open for 0% of the time, Pallas kernels for 0%

profile of v1, /device:TPU:0, one launch (start us, length us, event | category | flops | bytes accessed | tf_op | source)
XLA Modules:
  0.0 109.7 jit_solution(8145438438894719580)
XLA Ops:
  0.0 1.0 fusion.25
  1.0 0.8 fusion.27
  1.8 24.1 %all_gather.3 = bf16[128,1536]{1,0:T(8,128)(2,1)S(1)} all-gather(bf16[8,1536]{1,0:T(8,128)(2,1)S(1)} %fusion.27), channel_id=1, replica_groups=mesh['groups'=1,'tensor'=16,'replica'=2] {'tensor'}, dimensions={0}, use_global_device_ids=true | all-gather | bytes 417792 | tf_op jit(solution)/shard_map/all_gather | solution.py:301
  26.0 0.5 convolution_convert_fusion.1
  27.4 0.5 copy.50
  28.0 1.3 %reshape.207 = bf16[8,16,2304]{2,0,1:T(8,128)(2,1)} reshape(bf16[8,16,4,576]{3,2,0,1:T(4,128)(2,1)S(1)} %copy.50) | data formatting | bytes 1179648 | tf_op jit(solution)/shard_map/reshape | solution.py:310
  29.3 3.6 %all-to-all-start = ((bf16[8,16,2304]{2,0,1:T(8,128)(2,1)}), bf16[8,16,2304]{2,0,1:T(8,128)(2,1)S(1)}, u32[]{:S(2)}, u32[]{:S(2)}) async-start(bf16[8,16,2304]{2,0,1:T(8,128)(2,1)} %reshape.207), calls=%async_computation | async-start | bytes 1179648 | tf_op jit(solution)/shard_map/all_to_all | solution.py:313
  33.3 15.0 %all-to-all-done = bf16[8,16,2304]{2,0,1:T(8,128)(2,1)S(1)} async-done(((bf16[8,16,2304]{2,0,1:T(8,128)(2,1)}), bf16[8,16,2304]{2,0,1:T(8,128)(2,1)S(1)}, u32[]{:S(2)}, u32[]{:S(2)}) %all-to-all-start) | async-done | bytes 589856 | tf_op jit(solution)/shard_map/all_to_all | solution.py:313
  48.4 0.9 copy.38
  49.3 1.9 %reshape.199 = bf16[8,64,576]{2,1,0:T(8,128)(2,1)S(1)} reshape(bf16[8,16,2304]{2,1,0:T(8,128)(2,1)} %copy.38) | data formatting | bytes 1179648 | tf_op jit(solution)/shard_map/reshape | solution.py:314
  51.5 0.3 fusion.37
  51.8 1.0 copy-done.6
  52.8 1.1 fusion.2
  54.0 0.6 fusion.3
  54.5 0.4 fusion.28
  54.9 1.1 %fusion.10 = bf16[2,256,512]{2,1,0:T(8,128)(2,1)S(1)} fusion(f32[2,256,512]{2,1,0:T(8,128)S(1)} %fusion.28, bf16[2,1024,576]{1,2,0:T(8,128)(2,1)S(1)} %copy-done.6, f32[2,256,1024]{2,1,0:T(8,128)S(1)} %get-tuple-element.10, f32[2,256]{1,0:T(2,128)S(1)} %add.52, f32[2,256]{1,0:T(2,128)S(1)} %max.7, pred[2,1024]{1,0:T(4,128)(4,1)S(1)} %iota_compare_fusion, ...), kind=kOutput, calls=%fused_computation.10 | convolution fusion | flops 540278784 | bytes 5776384 | tf_op jit(solution)/shard_map/vmap()/dot_general | solution.py:72
  56.0 0.3 reshape.202
  56.3 0.3 copy.42
  56.6 18.6 %all_to_all.10 = bf16[8,16,2048]{2,0,1:T(8,128)(2,1)S(1)} all-to-all(bf16[8,16,2048]{2,0,1:T(8,128)(2,1)S(1)} %copy.42), channel_id=1, replica_groups=mesh['groups'=1,'tensor'=16,'replica'=2] {'tensor'}, dimensions={1} | all-to-all | bytes 1048576 | tf_op jit(solution)/shard_map/all_to_all | solution.py:327
  75.3 0.4 reshape.208
  75.7 1.7 %fusion.14 = bf16[16,8,4,128]{3,0,1,2:T(8,128)(2,1)S(1)} fusion(bf16[4,512,128]{2,1,0:T(8,128)(2,1)} %param.14, bf16[8,16,4,512]{3,2,0,1:T(4,128)(2,1)S(1)} %reshape.208), kind=kOutput, calls=%fused_computation.14 | convolution fusion | flops 67174400 | bytes 1179648 | tf_op jit(solution)/shard_map/ithl,hlv->tihv/dot_general | solution.py:329
  77.5 2.0 %copy-done.1 = bf16[512,3584]{1,0:T(8,128)(2,1)S(1)} copy-done((bf16[512,3584]{1,0:T(8,128)(2,1)S(1)}, bf16[512,3584]{1,0:T(8,128)(2,1)}, u32[]{:S(2)}) %copy-start.1) | copy-done | bytes 3670040
  79.5 29.6 %shard_map.100 = f32[2,8,3584]{2,1,0:T(8,128)S(1)} custom-call(bf16[128,512]{1,0:T(8,128)(2,1)S(1)} %bitcast.34, bf16[512,3584]{1,0:T(8,128)(2,1)S(1)} %copy-done.1), custom_call_target="tpu_custom_call" | custom-call | tf_op jit(solution)/shard_map/pallas_call | solution.py:263
  109.1 0.7 convert_element_type.70
  (37 shorter events, 1.8 us)
Async XLA Ops:
  0.0 26.0 %copy-start = (bf16[1536,768]{1,0:T(8,128)(2,1)S(1)}, bf16[1536,768]{1,0:T(8,128)(2,1)}, u32[]{:S(2)}) copy-start(bf16[1536,768]{1,0:T(8,128)(2,1)} %param.12) | copy-start | bytes 7077892
  26.0 1.0 copy-start.2
  27.4 5.5 %copy-start.5 = (s32[2]{0:T(128)S(1)}, s32[2]{0:T(128)}, u32[]{:S(2)}) copy-start(s32[2]{0:T(128)} %param.18) | copy-start | bytes 28
  27.4 5.6 %copy-start.3 = (bf16[8,576]{1,0:T(8,128)(2,1)S(1)}, bf16[8,576]{1,0:T(8,128)(2,1)}, u32[]{:S(2)}) copy-start(bf16[8,576]{1,0:T(8,128)(2,1)} %param.16) | copy-start | bytes 27652
  27.4 5.7 %copy-start.4 = (s32[2]{0:T(128)S(1)}, s32[2]{0:T(128)}, u32[]{:S(2)}) copy-start(s32[2]{0:T(128)} %param.19) | copy-start | bytes 28
  29.3 19.1 %all-to-all-start = ((bf16[8,16,2304]{2,0,1:T(8,128)(2,1)}), bf16[8,16,2304]{2,0,1:T(8,128)(2,1)S(1)}, u32[]{:S(2)}, u32[]{:S(2)}) async-start(bf16[8,16,2304]{2,0,1:T(8,128)(2,1)} %reshape.207), calls=%async_computation | async-start | bytes 1179648 | tf_op jit(solution)/shard_map/all_to_all | solution.py:313
  51.2 1.7 %copy-start.6 = (bf16[2,1024,576]{1,2,0:T(8,128)(2,1)S(1)}, bf16[2,1024,576]{1,2,0:T(8,128)(2,1)}, u32[]{:S(2)}) copy-start(bf16[2,1024,576]{1,2,0:T(8,128)(2,1)} %param.17) | copy-start | bytes 7077892
  77.4 2.0 %copy-start.1 = (bf16[512,3584]{1,0:T(8,128)(2,1)S(1)}, bf16[512,3584]{1,0:T(8,128)(2,1)}, u32[]{:S(2)}) copy-start(bf16[512,3584]{1,0:T(8,128)(2,1)} %wo_ref.1) | copy-start | bytes 11010052

commit v2 on v1

--- a/solution.py
+++ b/solution.py
@@ -18,63 +18,6 @@
 
 rms_eps = 1e-06
 rope_base = 50000.0
-
-
-def normalize(rows_in, gain_row):
-    values_f = rows_in.astype(jnp.float32)
-    scaled = values_f * lax.rsqrt(jnp.mean(values_f * values_f, axis=-1, keepdims=True) + rms_eps)
-    return (scaled * gain_row).astype(jnp.bfloat16)
-
-
-def rotate(rope_part, positions):
-    half_width = rope_part.shape[-1] // 2
-    frequency = rope_base ** (
-        -(jnp.arange(half_width).astype(jnp.float32) * 2.0 / rope_part.shape[-1])
-    )
-    angles = positions[:, None, None] * frequency
-    cosine = jnp.cos(angles)
-    sine = jnp.sin(angles)
-    widened = rope_part.astype(jnp.float32)
-    first_half = widened[..., :half_width]
-    second_half = widened[..., half_width:]
-    turned = jnp.concatenate(
-        [first_half * cosine - second_half * sine, second_half * cosine + first_half * sine],
-        axis=-1,
-    )
-    return turned.astype(jnp.bfloat16)
-
-
-def attend(query_rows, new_rows, cache_rows, length, draft_total):
-    queries = query_rows.reshape(-1, query_rows.shape[-1])
-    contract = (((1,), (1,)), ((), ()))
-    score_scale = (NOPE + ROPE) ** (-0.5)
-    cache_scores = (
-        lax.dot_general(queries, cache_rows, contract, preferred_element_type=jnp.float32)
-        * score_scale
-    )
-    new_scores = (
-        lax.dot_general(queries, new_rows, contract, preferred_element_type=jnp.float32)
-        * score_scale
-    )
-    row_draft = jnp.arange(queries.shape[0]) // query_rows.shape[1]
-    cache_seen = jnp.arange(cache_rows.shape[0]) < length
-    new_seen = jnp.arange(new_rows.shape[0])[None, :] <= row_draft[:, None]
-    cache_scores = jnp.where(cache_seen[None, :], cache_scores, -jnp.inf)
-    new_scores = jnp.where(new_seen, new_scores, -jnp.inf)
-    row_peak = jnp.maximum(jnp.max(cache_scores, axis=1), jnp.max(new_scores, axis=1))[:, None]
-    cache_exp = jnp.exp(cache_scores - row_peak)
-    new_exp = jnp.exp(new_scores - row_peak)
-    denominator = jnp.sum(cache_exp, axis=1, keepdims=True) + jnp.sum(
-        new_exp, axis=1, keepdims=True
-    )
-    cache_weights = (cache_exp / denominator).astype(jnp.bfloat16)
-    new_weights = (new_exp / denominator).astype(jnp.bfloat16)
-    latent_mix = jnp.dot(cache_weights, cache_rows[:, :LATENT], preferred_element_type=jnp.float32)
-    latent_mix = latent_mix + jnp.dot(
-        new_weights, new_rows[:, :LATENT], preferred_element_type=jnp.float32
-    )
-    latent_mix = jnp.where((row_draft < draft_total)[:, None], latent_mix, 0.0).astype(jnp.bfloat16)
-    return latent_mix.reshape(query_rows.shape[0], query_rows.shape[1], LATENT)
 
 
 def split_axis(count):
@@ -291,45 +234,273 @@
     )(head_values, w_o)
 
 
+def paired(first, second, low):
+    rows = first.shape[0]
+    zero = jnp.where(low, first, pltpu.roll(second, DRAFT, 0))
+    one = jnp.where(low, pltpu.roll(first, rows - DRAFT, 0), second)
+    return zero, one
+
+
+def mix(sizes, ql_ref, gain_ref, nk_ref, cos_ref, sin_ref, len_ref, count_ref, qup_hbm, wuk_hbm,
+        wuv_hbm, cache_hbm, hv_ref, qup, wuk, wuv, cache, gathered, qsend, rsend, qgot, rgot, lsend,
+        lgot, load_sem, fs, fr, ys, yr, ns, nr, qs, qr, rs, rr, ls, lr):
+    tensors = sizes
+    near, side, far = split_axis(tensors)
+    heads_dev = wuk.shape[0]
+    rows_dev = ql_ref.shape[0]
+    rows = tensors * rows_dev
+    half = ql_ref.shape[1] // 2
+    group, me, copy = place()
+    c = lax.rem(me, near)
+    y = lax.rem(me // near, side)
+    z = me // (near * side)
+    f32, bf16 = jnp.float32, jnp.bfloat16
+
+    loads = [
+        pltpu.make_async_copy(src, dst, load_sem.at[n])
+        for n, (src, dst) in enumerate(
+            ((qup_hbm, qup), (wuk_hbm, wuk), (cache_hbm, cache), (wuv_hbm, wuv))
+        )
+    ]
+    for load in loads:
+        load.start()
+
+    def peer(step):
+        return lax.rem(me + step, tensors)
+
+    def at(z_to, y_to, c_to):
+        return (group, (z_to * side + y_to) * near + c_to, copy)
+
+    def send(src, dst, send_sem, recv_sem, to):
+        push = pltpu.make_async_remote_copy(
+            src_ref=src, dst_ref=dst, send_sem=send_sem, recv_sem=recv_sem,
+            device_id=to, device_id_type=MESH,
+        )
+        push.start()
+        return push
+
+    values = ql_ref[...].astype(f32)
+    scaled = values * lax.rsqrt(jnp.mean(values * values, axis=-1, keepdims=True) + rms_eps)
+    normed = scaled * gain_ref[...]
+    gathered[c, y, z] = jnp.concatenate([normed[:, :half], normed[:, half:]], axis=0).astype(bf16)
+    meet([(group, peer(d), copy) for d in range(1, tensors)])
+
+    far_out = [
+        send(gathered.at[c, y, z], gathered.at[c, y, z], fs.at[d - 1], fr.at[d - 1],
+             at(lax.rem(z + d, far), y, c))
+        for d in range(1, far)
+    ]
+    for push in far_out:
+        push.wait_recv()
+    side_out = [
+        send(gathered.at[c, y], gathered.at[c, y], ys.at[d - 1], yr.at[d - 1],
+             at(z, lax.rem(y + d, side), c))
+        for d in range(1, side)
+    ]
+    for push in side_out:
+        push.wait_recv()
+    near_out = [
+        send(gathered.at[c], gathered.at[c], ns.at[d - 1], nr.at[d - 1],
+             at(z, y, lax.rem(c + d, near)))
+        for d in range(1, near)
+    ]
+    loads[0].wait()
+    loads[1].wait()
+    for push in near_out:
+        push.wait_recv()
+
+    everyone = gathered[...].astype(f32).reshape(tensors, 2 * rows_dev, half)
+    left = everyone[:, :rows_dev].reshape(rows, half).astype(bf16)
+    right = everyone[:, rows_dev:].reshape(rows, half).astype(bf16)
+    query = jnp.dot(left, qup[:half], preferred_element_type=f32)
+    query = query + jnp.dot(right, qup[half:], preferred_element_type=f32)
+    query = query.astype(bf16).astype(f32)
+    low = lax.broadcasted_iota(jnp.int32, (rows, 1), 0) % rows_dev < DRAFT
+    qkd = NOPE + ROPE
+    nope_pairs, rope_pairs = [], []
+    for h in range(0, heads_dev, 2):
+        here, there = h * qkd, (h + 1) * qkd
+        nope_pairs.append(
+            paired(query[:, here : here + NOPE], query[:, there : there + NOPE], low)
+        )
+        zero, one = paired(
+            query[:, here + NOPE : here + qkd], query[:, there + NOPE : there + qkd], low
+        )
+        rope_pairs.append(jnp.concatenate([zero, one], axis=1).reshape(tensors, rows_dev, 2 * ROPE))
+    rsend[...] = jnp.concatenate(rope_pairs, axis=1).astype(bf16)
+
+    def slot(to):
+        return (lax.rem(to, near) * side + lax.rem(to // near, side)) * far + to // (near * side)
+
+    mine = slot(me)
+    rope_out, query_out, latent_out = [], [], []
+    for r in range(REQ_DEV):
+        tiles = []
+        for n, pair in enumerate(nope_pairs):
+            tile = pair[r].astype(bf16)
+            first = jnp.dot(tile, wuk[2 * n], preferred_element_type=f32)
+            second = jnp.dot(tile, wuk[2 * n + 1], preferred_element_type=f32)
+            tiles.append(jnp.where(low, first, second).reshape(tensors, rows_dev, LATENT))
+        qsend[:, r] = jnp.concatenate(tiles, axis=1).astype(bf16)
+        for d in range(1, tensors):
+            to = peer(d)
+            if r == 0:
+                rope_out.append(
+                    send(rsend.at[slot(to)], rgot.at[me], rs.at[d - 1], rr.at[d - 1],
+                         (group, to, copy))
+                )
+            query_out.append(
+                send(qsend.at[slot(to), r], qgot.at[me, r], qs.at[r, d - 1], qr.at[r, d - 1],
+                     (group, to, copy))
+            )
+        qgot[me, r] = qsend[mine, r]
+    rgot[me] = rsend[mine]
+
+    pad = 128 - nk_ref.shape[0]
+    fresh = jnp.concatenate(
+        [nk_ref[...].astype(f32), jnp.zeros((pad, nk_ref.shape[1]), f32)], axis=0
+    ).astype(bf16)
+    fresh_latent, fresh_rope = fresh[:, :LATENT], fresh[:, LATENT:]
+    scale = qkd ** (-0.5)
+    total = tensors * heads_dev * DRAFT
+    slots = cache.shape[2]
+    row_draft = lax.broadcasted_iota(jnp.int32, (total, 1), 0) % DRAFT
+    fresh_column = lax.broadcasted_iota(jnp.int32, (1, 128), 1)
+    cache_column = lax.broadcasted_iota(jnp.int32, (1, slots), 1)
+    for push in rope_out:
+        push.wait_recv()
+    rope = rgot[...].astype(f32).reshape(total // rows_dev, rows_dev, 2 * ROPE)
+    rope2 = rope.reshape(total, 2 * ROPE)
+    lane = lax.broadcasted_iota(jnp.int32, (1, 2 * ROPE), 1) % ROPE
+    swapped = jnp.where(
+        lane < ROPE // 2,
+        pltpu.roll(rope2, 2 * ROPE - ROPE // 2, 1),
+        pltpu.roll(rope2, ROPE // 2, 1),
+    ).reshape(rope.shape)
+    turned = (rope * cos_ref[...][None] + swapped * sin_ref[...][None]).astype(bf16)
+    turned = turned.reshape(total, 2 * ROPE)
+    loads[2].wait()
+    transposed = (((1,), (1,)), ((), ()))
+    for r in range(REQ_DEV):
+        for push in query_out[r * (tensors - 1) : (r + 1) * (tensors - 1)]:
+            push.wait_recv()
+        absorbed = qgot[:, r].reshape(total, LATENT)
+        rotated = turned[:, r * ROPE : (r + 1) * ROPE]
+        scores = jnp.dot(absorbed, cache[r, :LATENT], preferred_element_type=f32)
+        scores = (scores + jnp.dot(rotated, cache[r, LATENT:], preferred_element_type=f32)) * scale
+        fresh_scores = lax.dot_general(
+            absorbed, fresh_latent, transposed, preferred_element_type=f32
+        )
+        fresh_scores = (
+            fresh_scores
+            + lax.dot_general(rotated, fresh_rope, transposed, preferred_element_type=f32)
+        ) * scale
+        scores = jnp.where(cache_column < len_ref[r], scores, -jnp.inf)
+        begin = r * DRAFT
+        seen = (fresh_column >= begin) & (fresh_column - begin <= row_draft)
+        fresh_scores = jnp.where(seen, fresh_scores, -jnp.inf)
+        peak = jnp.maximum(
+            jnp.max(scores, axis=1, keepdims=True), jnp.max(fresh_scores, axis=1, keepdims=True)
+        )
+        powers = jnp.exp(scores - peak)
+        fresh_powers = jnp.exp(fresh_scores - peak)
+        denominator = jnp.sum(powers, axis=1, keepdims=True) + jnp.sum(
+            fresh_powers, axis=1, keepdims=True
+        )
+        weights = (powers / denominator).astype(bf16)
+        fresh_weights = (fresh_powers / denominator).astype(bf16)
+        latents = lax.dot_general(
+            weights, cache[r, :LATENT], transposed, preferred_element_type=f32
+        )
+        latents = latents + jnp.dot(fresh_weights, fresh_latent, preferred_element_type=f32)
+        latents = jnp.where(row_draft < count_ref[r], latents, 0.0)
+        lsend[:, r] = latents.astype(bf16).reshape(tensors, heads_dev * DRAFT, LATENT)
+        for d in range(1, tensors):
+            to = peer(d)
+            latent_out.append(
+                send(lsend.at[to, r], lgot.at[me, r], ls.at[r, d - 1], lr.at[r, d - 1],
+                     (group, to, copy))
+            )
+        lgot[me, r] = lsend[me, r]
+    loads[3].wait()
+    halves = []
+    for r in range(REQ_DEV):
+        for push in latent_out[r * (tensors - 1) : (r + 1) * (tensors - 1)]:
+            push.wait_recv()
+        back = lgot[:, r].astype(f32)
+        parts = []
+        for n in range(heads_dev // 2):
+            tile = back[:, n * rows_dev : (n + 1) * rows_dev].reshape(rows, LATENT).astype(bf16)
+            first = jnp.dot(tile, wuv[2 * n], preferred_element_type=f32)
+            second = jnp.dot(tile, wuv[2 * n + 1], preferred_element_type=f32)
+            parts.append(jnp.where(low, first, second))
+        halves.append(parts)
+    for n in range(heads_dev // 2):
+        for h, block in enumerate(paired(halves[0][n], halves[1][n], low)):
+            start = (2 * n + h) * VDIM
+            hv_ref[:, start : start + VDIM] = block.astype(bf16)
+    for push in far_out + side_out + near_out + rope_out + query_out + latent_out:
+        push.wait_send()
+
+
+def mix_call(q_latent, q_gain, q_up, w_uk, w_uv, new_kv, latent_cache, cache_len, draft_count, tensors):
+    near, side, far = split_axis(tensors)
+    rows_dev, width = q_latent.shape
+    heads_dev = w_uk.shape[0]
+    bf16, f32 = jnp.bfloat16, jnp.float32
+    dma = pltpu.SemaphoreType.DMA
+    n1, n2, n3 = (max(v - 1, 1) for v in (near, side, far))
+    tall = heads_dev * DRAFT
+    cache = jnp.swapaxes(latent_cache, 1, 2)
+    frequency = rope_base ** (-(jnp.arange(ROPE // 2).astype(f32) * 2.0 / ROPE))
+    positions = (cache_len[:, None] + jnp.arange(DRAFT)).astype(f32)
+    angles = positions[:, :, None] * frequency
+    cosine, sine = jnp.cos(angles), jnp.sin(angles)
+    cosine = jnp.concatenate([cosine, cosine], axis=-1)
+    sine = jnp.concatenate([-sine, sine], axis=-1)
+    lay = lambda a: jnp.tile(jnp.swapaxes(a, 0, 1).reshape(DRAFT, REQ_DEV * ROPE), (2, 1))
+    vmem = pl.BlockSpec(memory_space=pltpu.VMEM)
+    smem = pl.BlockSpec(memory_space=pltpu.SMEM)
+    hbm = pl.BlockSpec(memory_space=pl.ANY)
+    exchange = (REQ_DEV, tensors - 1)
+    return pl.pallas_call(
+        functools.partial(mix, tensors),
+        out_shape=jax.ShapeDtypeStruct((tensors * rows_dev, heads_dev * VDIM), bf16),
+        in_specs=[vmem] * 5 + [smem] * 2 + [hbm] * 4,
+        out_specs=vmem,
+        scratch_shapes=[
+            pltpu.VMEM(q_up.shape, bf16),
+            pltpu.VMEM(w_uk.shape, bf16),
+            pltpu.VMEM(w_uv.shape, bf16),
+            pltpu.VMEM(cache.shape, bf16),
+            pltpu.VMEM((near, side, far, 2 * rows_dev, width // 2), bf16),
+            pltpu.VMEM((tensors, REQ_DEV, tall, LATENT), bf16),
+            pltpu.VMEM((tensors, tall, 2 * ROPE), bf16),
+            pltpu.VMEM((tensors, REQ_DEV, tall, LATENT), bf16),
+            pltpu.VMEM((tensors, tall, 2 * ROPE), bf16),
+            pltpu.VMEM((tensors, REQ_DEV, tall, LATENT), bf16),
+            pltpu.VMEM((tensors, REQ_DEV, tall, LATENT), bf16),
+            dma((4,)),
+            dma((n3,)), dma((n3,)),
+            dma((n2,)), dma((n2,)),
+            dma((n1,)), dma((n1,)),
+            dma(exchange), dma(exchange),
+            dma((tensors - 1,)), dma((tensors - 1,)),
+            dma(exchange), dma(exchange),
+        ],
+        compiler_params=pltpu.CompilerParams(
+            collective_id=1, has_side_effects=True, vmem_limit_bytes=48 * 1024 * 1024
+        ),
+    )(q_latent, q_gain[None], new_kv, lay(cosine), lay(sine), cache_len, draft_count,
+      q_up, w_uk, w_uv, cache)
+
+
 def shards(q_latent, q_gain, q_up, w_uk, w_uv, w_o, new_kv, latent_cache, cache_len, draft_count):
     rows_dev = q_latent.shape[0]
     owners = lax.axis_size("tensor")
-    heads_dev = w_uk.shape[0]
-    head_count = heads_dev * owners
-    normed = normalize(q_latent, q_gain)
-    query_full = jnp.dot(
-        lax.all_gather(normed, "tensor", axis=0, tiled=True),
-        q_up,
-        preferred_element_type=jnp.float32,
-    ).astype(jnp.bfloat16)
-    query_full = query_full.reshape(owners, rows_dev, heads_dev, NOPE + ROPE)
-    absorbed = jnp.einsum(
-        "pihn,hnl->iphl", query_full[..., :NOPE], w_uk, preferred_element_type=jnp.float32
-    ).astype(jnp.bfloat16)
-    rope_part = jnp.swapaxes(query_full[..., NOPE:], 0, 1)
-    packed_queries = jnp.concatenate([absorbed, rope_part], axis=-1).reshape(
-        rows_dev, owners, heads_dev * (LATENT + ROPE)
+    head_values = mix_call(
+        q_latent, q_gain, q_up, w_uk, w_uv, new_kv, latent_cache, cache_len, draft_count, owners
     )
-    arrived = lax.all_to_all(packed_queries, "tensor", split_axis=1, concat_axis=1, tiled=True)
-    arrived = arrived.reshape(rows_dev, head_count, LATENT + ROPE)
-    row_length = jnp.broadcast_to(cache_len[:, None], (REQ_DEV, DRAFT)).reshape(-1)
-    positions = (row_length + jnp.arange(rows_dev) % DRAFT).astype(jnp.float32)
-    rotated = rotate(arrived[..., LATENT:], positions)
-    query = jnp.concatenate([arrived[..., :LATENT], rotated], axis=-1)
-    latent_out = jax.vmap(attend)(
-        query.reshape(REQ_DEV, DRAFT, head_count, LATENT + ROPE),
-        new_kv.reshape(REQ_DEV, DRAFT, LATENT + ROPE),
-        latent_cache,
-        cache_len,
-        draft_count,
-    )
-    latent_out = latent_out.reshape(rows_dev, owners, heads_dev * LATENT)
-    returned = lax.all_to_all(latent_out, "tensor", split_axis=1, concat_axis=1, tiled=True)
-    returned = returned.reshape(rows_dev, owners, heads_dev, LATENT)
-    head_values = jnp.einsum(
-        "ithl,hlv->tihv", returned, w_uv, preferred_element_type=jnp.float32
-    ).astype(jnp.bfloat16)
-    head_values = head_values.reshape(owners * rows_dev, heads_dev * VDIM)
     replicas = lax.axis_size("replica")
     placed = project_call(head_values, w_o, owners, replicas, rows_dev)
     placed = jnp.swapaxes(placed, 0, 1).reshape(rows_dev, replicas * w_o.shape[1])

time: 110 us -> 85.3 us (0.78)
  Pallas kernels: 29.6 us -> 74.2 us
  blocking collectives: 42.8 us -> 0 us
  waiting for transfers between devices: 15 us -> 0 us
  matrix products: 5.33 us -> 0 us
  starting transfers between devices: 3.58 us -> 0 us
  other arithmetic: 3.73 us -> 1.55 us
    pallas_call x0 -> x1, Pallas kernels: none -> 41.8 us  [mix_call(): pl.pallas_call(functools.partial(mix, tensors), out_shape=jax.ShapeDtypeS...]
    all_gather x1 -> x0, blocking collectives: 24.1 us -> none  [shards(): lax.all_gather(normed, 'tensor', axis=0, tiled=True)]
    all_to_all x1 -> x0, blocking collectives: 18.6 us -> none  [shards(): lax.all_to_all(latent_out, 'tensor', split_axis=1, concat_axis=1, tiled=T...]
    all_to_all x1 -> x0, waiting for transfers between devices: 15 us -> none  [shards(): lax.all_to_all(packed_queries, 'tensor', split_axis=1, concat_axis=1, til...]
    dot_general x7 -> x0, matrix products: 5.33 us -> none  [the longest x1 1.74 us: shards(): jnp.einsum('ithl,hlv->tihv', returned, w_uv, preferred_element_type=jnp.f...]
    reshape x9 -> x0, local copies, waits for them, and re-layouts: 5.05 us -> none  [the longest x1 1.9 us: shards(): arrived = arrived.reshape(rows_dev, head_count, LATENT + ROPE)]
    unnamed x15 -> x18, local copies, waits for them, and re-layouts: 3.24 us -> 8.17 us
    all_to_all x1 -> x0, starting transfers between devices: 3.58 us -> none  [shards(): lax.all_to_all(packed_queries, 'tensor', split_axis=1, concat_axis=1, til...]
  transfers between devices with their start and end apart: 1 -> 0, of which waited for: 1 -> 0; matrix products, arithmetic and copies ran while one was open for 0% -> 0% of each run, Pallas kernels for 0% -> 0%
where the time goes in v2:
time: 85.3 us; the launch traced here: 84.9 us
  Pallas kernels  74.2 us (87%)
  local copies, waits for them, and re-layouts  9.05 us (11%)
  other arithmetic  1.55 us (2%)
    pallas_call x1, Pallas kernels, mix_call(): pl.pallas_call(functools.partial(mix, tensors), out_shape=jax.ShapeDtypeS...  41.8 us
    pallas_call x1, Pallas kernels, project_call(): pl.pallas_call(functools.partial(project, (tensors, copies, rows_dev)), o...  32.4 us
    unnamed x18, local copies, waits for them, and re-layouts  8.17 us

profile of v2, /device:TPU:0, one launch (start us, length us, event | category | flops | bytes accessed | tf_op | source)
XLA Modules:
  0.0 84.9 jit_solution(17003699512488244620)
XLA Ops:
  0.0 0.7 add_convert_fusion
  0.7 0.7 broadcast_in_dim.2.gain_ref
  1.4 0.1 fusion
  1.5 0.1 maximum_bitcast_fusion
  1.6 0.1 tile.20
  1.7 0.1 tile.23
  1.8 0.0 copy-start.1
  1.8 1.7 %copy-done.1 = bf16[1536,768]{1,0:T(8,128)(2,1)S(1)} copy-done((bf16[1536,768]{1,0:T(8,128)(2,1)S(1)}, bf16[1536,768]{1,0:T(8,128)(2,1)}, u32[]{:S(2)}) %copy-start.1) | copy-done | bytes 2359320
  3.4 0.0 copy-start.2
  3.5 1.7 %copy-done.2 = bf16[2,1024,576]{1,2,0:T(8,128)(2,1)S(1)} copy-done((bf16[2,1024,576]{1,2,0:T(8,128)(2,1)S(1)}, bf16[2,1024,576]{1,2,0:T(8,128)(2,1)}, u32[]{:S(2)}) %copy-start.2) | copy-done | bytes 2359320
  5.1 0.0 copy-start.3
  5.1 1.0 %copy-done.3 = bf16[4,128,512]{2,1,0:T(8,128)(2,1)S(1)} copy-done((bf16[4,128,512]{2,1,0:T(8,128)(2,1)S(1)}, bf16[4,128,512]{2,1,0:T(8,128)(2,1)}, u32[]{:S(2)}) %copy-start.3) | copy-done | bytes 524312
  6.2 0.0 copy-start.4
  6.2 1.0 %copy-done.4 = bf16[4,512,128]{2,1,0:T(8,128)(2,1)S(1)} copy-done((bf16[4,512,128]{2,1,0:T(8,128)(2,1)S(1)}, bf16[4,512,128]{2,1,0:T(8,128)(2,1)}, u32[]{:S(2)}) %copy-start.4) | copy-done | bytes 524312
  7.2 0.0 copy-start.5
  7.2 0.7 copy-done.5
  7.9 0.0 copy-start.6
  7.9 0.7 copy-done.6
  8.6 0.7 copy-done.7
  9.3 0.7 copy-done.8
  10.0 41.8 %shard_map.100.hv_ref = bf16[128,512]{1,0:T(8,128)(2,1)S(1)} custom-call(bf16[8,1536]{1,0:T(8,128)(2,1)S(1)} %copy-done.5, f32[1,1536]{1,0:T(1,128)S(1)} %broadcast_in_dim.2.gain_ref, bf16[8,576]{1,0:T(8,128)(2,1)S(1)} %copy-done.6, f32[8,128]{1,0:T(8,128)S(1)} %bitcast.11, f32[8,128]{1,0:T(8,128)S(1)} %bitcast.12, s32[2]{0:T(128)S(1)} %copy-done.7, ...), custom_call_target="tpu_custom_call" | custom-call | tf_op jit(solution)/shard_map/pallas_call | solution.py:466
  51.8 0.0 copy-done
  51.8 32.4 %shard_map.101 = f32[2,8,3584]{2,1,0:T(8,128)S(1)} custom-call(bf16[128,512]{1,0:T(8,128)(2,1)S(1)} %shard_map.100.hv_ref, bf16[512,3584]{1,0:T(8,128)(2,1)S(1)} %copy-done), custom_call_target="tpu_custom_call" | custom-call | tf_op jit(solution)/shard_map/pallas_call | solution.py:206
  84.2 0.7 convert_element_type.25
  (6 shorter events, 0.0 us)
Async XLA Ops:
  1.8 1.7 %copy-start.1 = (bf16[1536,768]{1,0:T(8,128)(2,1)S(1)}, bf16[1536,768]{1,0:T(8,128)(2,1)}, u32[]{:S(2)}) copy-start(bf16[1536,768]{1,0:T(8,128)(2,1)} %qup_hbm.1) | copy-start | bytes 7077892
  3.4 1.7 %copy-start.2 = (bf16[2,1024,576]{1,2,0:T(8,128)(2,1)S(1)}, bf16[2,1024,576]{1,2,0:T(8,128)(2,1)}, u32[]{:S(2)}) copy-start(bf16[2,1024,576]{1,2,0:T(8,128)(2,1)} %param.17) | copy-start | bytes 7077892
  5.1 1.0 %copy-start.3 = (bf16[4,128,512]{2,1,0:T(8,128)(2,1)S(1)}, bf16[4,128,512]{2,1,0:T(8,128)(2,1)}, u32[]{:S(2)}) copy-start(bf16[4,128,512]{2,1,0:T(8,128)(2,1)} %wuk_hbm.1) | copy-start | bytes 1572868
  6.2 1.0 %copy-start.4 = (bf16[4,512,128]{2,1,0:T(8,128)(2,1)S(1)}, bf16[4,512,128]{2,1,0:T(8,128)(2,1)}, u32[]{:S(2)}) copy-start(bf16[4,512,128]{2,1,0:T(8,128)(2,1)} %wuv_hbm.1) | copy-start | bytes 1572868
  7.2 0.7 copy-start.5
  7.9 0.7 copy-start.6
  8.6 0.7 copy-start.7
  9.3 0.7 copy-start.8
  10.0 41.8 %copy-start = (bf16[512,3584]{1,0:T(8,128)(2,1)S(1)}, bf16[512,3584]{1,0:T(8,128)(2,1)}, u32[]{:S(2)}) copy-start(bf16[512,3584]{1,0:T(8,128)(2,1)} %wo_ref.1) | copy-start | bytes 11010052

commit v3 on v2

--- a/solution.py
+++ b/solution.py
@@ -1,4 +1,5 @@
 import functools
+import math
 
 import jax
 import jax.numpy as jnp
@@ -27,7 +28,7 @@
 
 
 def column_chunks(width):
-    for parts in (4, 3, 2):
+    for parts in (7, 4, 3, 2):
         if width % (parts * 128) == 0:
             return parts
     return 1
@@ -47,8 +48,8 @@
     return group, me, copy
 
 
-def project(sizes, hv_ref, wo_ref, out_ref, spread, wo, sent1, got1, sent2, got2, kept2, sent3,
-            got3, kept3, sentx, gotx, wo_sem, hs, hr, s1, r1, s2, r2, s3, r3, sx, rx):
+def project(sizes, loads, hv_ref, wo_ref, out_ref, spread, wo, sent1, got1, sent2, got2, kept2, sent3,
+            got3, kept3, sentx, gotx, hs, hr, s1, r1, s2, r2, s3, r3, sx, rx):
     tensors, copies, rows_dev = sizes
     near, side, far = split_axis(tensors)
     parts = column_chunks(wo_ref.shape[1])
@@ -64,20 +65,10 @@
     def twin(step):
         return lax.rem(copy + step, copies)
 
-    loads = [
-        pltpu.make_async_copy(
-            wo_ref.at[:, pl.ds(k * width, width)], wo.at[k], wo_sem.at[k]
-        )
-        for k in range(parts)
-    ]
-    for load in loads:
-        load.start()
     near_peers = [at(z, y, lax.rem(c + d, near)) for d in range(1, near)]
     side_peers = [at(z, lax.rem(y + d, side), c) for d in range(1, side)]
     far_peers = [at(lax.rem(z + d, far), y, c) for d in range(1, far)]
     twin_peers = [(group, me, twin(d)) for d in range(1, copies)]
-    meet(near_peers + side_peers + far_peers + twin_peers)
-
     def send(src, dst, send_sem, recv_sem, peer):
         push = pltpu.make_async_remote_copy(
             src_ref=src, dst_ref=dst, send_sem=send_sem, recv_sem=recv_sem,
@@ -195,22 +186,17 @@
                 push.wait_send()
 
 
-def project_call(head_values, w_o, tensors, copies, rows_dev):
+def project_scratch(hv_shape, wo_shape, tensors, copies, rows_dev):
     near, side, far = split_axis(tensors)
-    parts = column_chunks(w_o.shape[1])
-    width = w_o.shape[1] // parts
+    parts = column_chunks(wo_shape[1])
+    width = wo_shape[1] // parts
     block = copies * rows_dev
     bf16, f32 = jnp.bfloat16, jnp.float32
     dma = pltpu.SemaphoreType.DMA
     n1, n2, n3, nx = (max(v - 1, 1) for v in (near, side, far, copies))
-    return pl.pallas_call(
-        functools.partial(project, (tensors, copies, rows_dev)),
-        out_shape=jax.ShapeDtypeStruct((copies, rows_dev, w_o.shape[1]), f32),
-        in_specs=[pl.BlockSpec(memory_space=pltpu.VMEM), pl.BlockSpec(memory_space=pl.ANY)],
-        out_specs=pl.BlockSpec(memory_space=pltpu.VMEM),
-        scratch_shapes=[
-            pltpu.VMEM((nx,) + head_values.shape, bf16),
-            pltpu.VMEM((parts, w_o.shape[0], width), bf16),
+    return [
+            pltpu.VMEM((nx,) + hv_shape, bf16),
+            pltpu.VMEM((parts, wo_shape[0], width), bf16),
             pltpu.VMEM((parts, near, side, far, block, width), bf16),
             pltpu.VMEM((parts, n1, side, far, block, width), bf16),
             pltpu.VMEM((parts, n2, far, block, width), bf16),
@@ -221,17 +207,12 @@
             pltpu.VMEM((parts, block, width), f32),
             pltpu.VMEM((parts, copies, rows_dev, width), f32),
             pltpu.VMEM((parts, nx, rows_dev, width), f32),
-            dma((parts,)),
             dma((nx,)), dma((nx,)),
             dma((parts, n1)), dma((parts, n1)),
             dma((parts, n2)), dma((parts, n2)),
             dma((parts, n3)), dma((parts, n3)),
             dma((parts, nx)), dma((parts, nx)),
-        ],
-        compiler_params=pltpu.CompilerParams(
-            collective_id=3, has_side_effects=True, vmem_limit_bytes=48 * 1024 * 1024
-        ),
-    )(head_values, w_o)
+    ]
 
 
 def paired(first, second, low):
@@ -241,13 +222,13 @@
     return zero, one
 
 
-def mix(sizes, ql_ref, gain_ref, nk_ref, cos_ref, sin_ref, len_ref, count_ref, qup_hbm, wuk_hbm,
-        wuv_hbm, cache_hbm, hv_ref, qup, wuk, wuv, cache, gathered, qsend, rsend, qgot, rgot, lsend,
-        lgot, load_sem, fs, fr, ys, yr, ns, nr, qs, qr, rs, rr, ls, lr):
-    tensors = sizes
+def mix(sizes, gain_ref, ql_ref, nk_ref, len_ref, count_ref, qup_hbm, wuk_hbm, wuv_hbm, cache_hbm,
+        wo_hbm, out_ref, qup, wuk, wuv, cache, hv_ref, gathered,
+        qsend, rsend, qgot, rgot, lsend, lgot, load_sem, wo_sem, fs, fr, ys, yr, ns, nr, qs, qr, rs,
+        rr, ls, lr, *rest):
+    tensors, copies, rows_dev = sizes
     near, side, far = split_axis(tensors)
     heads_dev = wuk.shape[0]
-    rows_dev = ql_ref.shape[0]
     rows = tensors * rows_dev
     half = ql_ref.shape[1] // 2
     group, me, copy = place()
@@ -262,7 +243,13 @@
             ((qup_hbm, qup), (wuk_hbm, wuk), (cache_hbm, cache), (wuv_hbm, wuv))
         )
     ]
-    for load in loads:
+    wo = rest[1]
+    width = wo.shape[2]
+    wo_loads = [
+        pltpu.make_async_copy(wo_hbm.at[:, pl.ds(k * width, width)], wo.at[k], wo_sem.at[k])
+        for k in range(wo.shape[0])
+    ]
+    for load in loads + wo_loads:
         load.start()
 
     def peer(step):
@@ -283,13 +270,25 @@
     scaled = values * lax.rsqrt(jnp.mean(values * values, axis=-1, keepdims=True) + rms_eps)
     normed = scaled * gain_ref[...]
     gathered[c, y, z] = jnp.concatenate([normed[:, :half], normed[:, half:]], axis=0).astype(bf16)
-    meet([(group, peer(d), copy) for d in range(1, tensors)])
+    meet(
+        [(group, peer(d), copy) for d in range(1, tensors)]
+        + [(group, me, lax.rem(copy + d, copies)) for d in range(1, copies)]
+    )
 
     far_out = [
         send(gathered.at[c, y, z], gathered.at[c, y, z], fs.at[d - 1], fr.at[d - 1],
              at(lax.rem(z + d, far), y, c))
         for d in range(1, far)
     ]
+    column = lax.broadcasted_iota(jnp.int32, (rows_dev, 2 * ROPE), 1)
+    table_draft = lax.broadcasted_iota(jnp.int32, (rows_dev, 2 * ROPE), 0) % DRAFT
+    fraction = (column % (ROPE // 2)).astype(f32) * 2.0 / ROPE
+    frequency = jnp.exp(fraction * -math.log(rope_base))
+    length = jnp.where(column < ROPE, len_ref[0], len_ref[1])
+    angle = (length + table_draft).astype(f32) * frequency
+    cosine = jnp.cos(angle)
+    sine = jnp.sin(angle)
+    sine = jnp.where(column % ROPE < ROPE // 2, -sine, sine)
     for push in far_out:
         push.wait_recv()
     side_out = [
@@ -377,7 +376,7 @@
         pltpu.roll(rope2, 2 * ROPE - ROPE // 2, 1),
         pltpu.roll(rope2, ROPE // 2, 1),
     ).reshape(rope.shape)
-    turned = (rope * cos_ref[...][None] + swapped * sin_ref[...][None]).astype(bf16)
+    turned = (rope * cosine[None] + swapped * sine[None]).astype(bf16)
     turned = turned.reshape(total, 2 * ROPE)
     loads[2].wait()
     transposed = (((1,), (1,)), ((), ()))
@@ -439,11 +438,13 @@
         for h, block in enumerate(paired(halves[0][n], halves[1][n], low)):
             start = (2 * n + h) * VDIM
             hv_ref[:, start : start + VDIM] = block.astype(bf16)
+    project(sizes, wo_loads, hv_ref, wo_hbm, out_ref, *rest)
     for push in far_out + side_out + near_out + rope_out + query_out + latent_out:
         push.wait_send()
 
 
-def mix_call(q_latent, q_gain, q_up, w_uk, w_uv, new_kv, latent_cache, cache_len, draft_count, tensors):
+def mix_call(q_latent, q_gain, q_up, w_uk, w_uv, w_o, new_kv, latent_cache, cache_len, draft_count,
+             tensors, copies):
     near, side, far = split_axis(tensors)
     rows_dev, width = q_latent.shape
     heads_dev = w_uk.shape[0]
@@ -452,27 +453,21 @@
     n1, n2, n3 = (max(v - 1, 1) for v in (near, side, far))
     tall = heads_dev * DRAFT
     cache = jnp.swapaxes(latent_cache, 1, 2)
-    frequency = rope_base ** (-(jnp.arange(ROPE // 2).astype(f32) * 2.0 / ROPE))
-    positions = (cache_len[:, None] + jnp.arange(DRAFT)).astype(f32)
-    angles = positions[:, :, None] * frequency
-    cosine, sine = jnp.cos(angles), jnp.sin(angles)
-    cosine = jnp.concatenate([cosine, cosine], axis=-1)
-    sine = jnp.concatenate([-sine, sine], axis=-1)
-    lay = lambda a: jnp.tile(jnp.swapaxes(a, 0, 1).reshape(DRAFT, REQ_DEV * ROPE), (2, 1))
     vmem = pl.BlockSpec(memory_space=pltpu.VMEM)
-    smem = pl.BlockSpec(memory_space=pltpu.SMEM)
-    hbm = pl.BlockSpec(memory_space=pl.ANY)
+    hbm = pl.BlockSpec(memory_space=pltpu.HBM)
+    hv_shape = (tensors * rows_dev, heads_dev * VDIM)
     exchange = (REQ_DEV, tensors - 1)
     return pl.pallas_call(
-        functools.partial(mix, tensors),
-        out_shape=jax.ShapeDtypeStruct((tensors * rows_dev, heads_dev * VDIM), bf16),
-        in_specs=[vmem] * 5 + [smem] * 2 + [hbm] * 4,
+        functools.partial(mix, (tensors, copies, rows_dev)),
+        out_shape=jax.ShapeDtypeStruct((copies, rows_dev, w_o.shape[1]), f32),
+        in_specs=[vmem] * 3 + [pl.BlockSpec(memory_space=pltpu.SMEM)] * 2 + [hbm] * 5,
         out_specs=vmem,
         scratch_shapes=[
             pltpu.VMEM(q_up.shape, bf16),
             pltpu.VMEM(w_uk.shape, bf16),
             pltpu.VMEM(w_uv.shape, bf16),
             pltpu.VMEM(cache.shape, bf16),
+            pltpu.VMEM(hv_shape, bf16),
             pltpu.VMEM((near, side, far, 2 * rows_dev, width // 2), bf16),
             pltpu.VMEM((tensors, REQ_DEV, tall, LATENT), bf16),
             pltpu.VMEM((tensors, tall, 2 * ROPE), bf16),
@@ -481,28 +476,29 @@
             pltpu.VMEM((tensors, REQ_DEV, tall, LATENT), bf16),
             pltpu.VMEM((tensors, REQ_DEV, tall, LATENT), bf16),
             dma((4,)),
+            dma((column_chunks(w_o.shape[1]),)),
             dma((n3,)), dma((n3,)),
             dma((n2,)), dma((n2,)),
             dma((n1,)), dma((n1,)),
             dma(exchange), dma(exchange),
             dma((tensors - 1,)), dma((tensors - 1,)),
             dma(exchange), dma(exchange),
-        ],
+        ]
+        + project_scratch(hv_shape, w_o.shape, tensors, copies, rows_dev),
         compiler_params=pltpu.CompilerParams(
-            collective_id=1, has_side_effects=True, vmem_limit_bytes=48 * 1024 * 1024
+            collective_id=1, has_side_effects=True, vmem_limit_bytes=56 * 1024 * 1024
         ),
-    )(q_latent, q_gain[None], new_kv, lay(cosine), lay(sine), cache_len, draft_count,
-      q_up, w_uk, w_uv, cache)
+    )(q_gain[None], q_latent, new_kv, cache_len, draft_count, q_up, w_uk, w_uv, cache, w_o)
 
 
 def shards(q_latent, q_gain, q_up, w_uk, w_uv, w_o, new_kv, latent_cache, cache_len, draft_count):
     rows_dev = q_latent.shape[0]
     owners = lax.axis_size("tensor")
-    head_values = mix_call(
-        q_latent, q_gain, q_up, w_uk, w_uv, new_kv, latent_cache, cache_len, draft_count, owners
+    replicas = lax.axis_size("replica")
+    placed = mix_call(
+        q_latent, q_gain, q_up, w_uk, w_uv, w_o, new_kv, latent_cache, cache_len, draft_count,
+        owners, replicas
     )
-    replicas = lax.axis_size("replica")
-    placed = project_call(head_values, w_o, owners, replicas, rows_dev)
     placed = jnp.swapaxes(placed, 0, 1).reshape(rows_dev, replicas * w_o.shape[1])
     return placed.astype(jnp.bfloat16)
 

time: 85.3 us -> 80.6 us (0.945)
  local copies, waits for them, and re-layouts: 9.05 us -> 1.29 us
  Pallas kernels: 74.2 us -> 77.4 us
    unnamed x18 -> x0, local copies, waits for them, and re-layouts: 8.17 us -> none
    pallas_call x2 -> x1, Pallas kernels: 74.2 us -> 77.4 us  [mix_call(): pl.pallas_call(functools.partial(mix, (tensors, copies, rows_dev)), out_s...]
    convert_element_type x1, other arithmetic: 0.66 us -> 1.6 us  [shards(): return placed.astype(jnp.bfloat16)]
where the time goes in v3:
time: 80.6 us; the launch traced here: 80.3 us
  Pallas kernels  77.4 us (96%)
  other arithmetic  1.6 us (2%)
  local copies, waits for them, and re-layouts  1.29 us (2%)
    pallas_call x1, Pallas kernels, mix_call(): pl.pallas_call(functools.partial(mix, (tensors, copies, rows_dev)), out_s...  77.4 us

profile of v3, /device:TPU:0, one launch (start us, length us, event | category | flops | bytes accessed | tf_op | source)
XLA Modules:
  0.0 80.3 jit_solution(2792257489275457220)
XLA Ops:
  0.0 1.3 %broadcast_in_dim.3.gain_ref = f32[1,1536]{1,0:T(1,128)} reshape(f32[1536]{0:T(1024)} %param.11) | data formatting | bytes 12288 | tf_op jit(solution)/shard_map/broadcast_in_dim | solution.py:491
  1.3 77.4 %shard_map.100 = f32[2,8,3584]{2,1,0:T(8,128)} custom-call(f32[1,1536]{1,0:T(1,128)} %broadcast_in_dim.3.gain_ref, bf16[8,1536]{1,0:T(8,128)(2,1)} %ql_ref.1, bf16[8,576]{1,0:T(8,128)(2,1)} %nk_ref.1, s32[2]{0:T(128)} %len_ref.1, s32[2]{0:T(128)} %count_ref.1, bf16[1536,768]{1,0:T(8,128)(2,1)} %qup_hbm.1, bf16[4,128,512]{2,1,0:T(8,128)(2,1)} %wuk_hbm.1, ...), custom_call_target="tpu_custom_call" | custom-call | tf_op jit(solution)/shard_map/pallas_call | solution.py:460
  78.7 1.6 %convert_element_type.9 = bf16[2,8,3584]{2,1,0:T(8,128)(2,1)} convert(f32[2,8,3584]{2,1,0:T(8,128)} %shard_map.100) | non-fusion elementwise | flops 57344 | bytes 344064 | tf_op jit(solution)/shard_map/convert_element_type | solution.py:503

commit v4 on v3

--- a/solution.py
+++ b/solution.py
@@ -28,7 +28,7 @@
 
 
 def column_chunks(width):
-    for parts in (7, 4, 3, 2):
+    for parts in (4, 3, 2):
         if width % (parts * 128) == 0:
             return parts
     return 1
@@ -268,7 +268,7 @@
 
     values = ql_ref[...].astype(f32)
     scaled = values * lax.rsqrt(jnp.mean(values * values, axis=-1, keepdims=True) + rms_eps)
-    normed = scaled * gain_ref[...]
+    normed = scaled * gain_ref[...].reshape(1, 2 * half)
     gathered[c, y, z] = jnp.concatenate([normed[:, :half], normed[:, half:]], axis=0).astype(bf16)
     meet(
         [(group, peer(d), copy) for d in range(1, tensors)]
@@ -488,7 +488,7 @@
         compiler_params=pltpu.CompilerParams(
             collective_id=1, has_side_effects=True, vmem_limit_bytes=56 * 1024 * 1024
         ),
-    )(q_gain[None], q_latent, new_kv, cache_len, draft_count, q_up, w_uk, w_uv, cache, w_o)
+    )(q_gain, q_latent, new_kv, cache_len, draft_count, q_up, w_uk, w_uv, cache, w_o)
 
 
 def shards(q_latent, q_gain, q_up, w_uk, w_uv, w_o, new_kv, latent_cache, cache_len, draft_count):

time: 80.6 us -> 73.6 us (0.913)
  Pallas kernels: 77.4 us -> 71.8 us
  local copies, waits for them, and re-layouts: 1.29 us -> 0 us
    pallas_call x1, Pallas kernels: 77.4 us -> 71.8 us  [mix_call(): pl.pallas_call(functools.partial(mix, (tensors, copies, rows_dev)), out_s...]
    broadcast_in_dim x1 -> x0, local copies, waits for them, and re-layouts: 1.29 us -> none  [mix_call(): q_gain[None]]
where the time goes in v4:
time: 73.6 us; the launch traced here: 73.4 us
  Pallas kernels  71.8 us (98%)
  other arithmetic  1.6 us (2%)
    pallas_call x1, Pallas kernels, mix_call(): pl.pallas_call(functools.partial(mix, (tensors, copies, rows_dev)), out_s...  71.8 us
    convert_element_type x1, other arithmetic, shards(): return placed.astype(jnp.bfloat16)  1.6 us

profile of v4, /device:TPU:0, one launch (start us, length us, event | category | flops | bytes accessed | tf_op | source)
XLA Modules:
  0.0 73.4 jit_solution(17438670337843648730)
XLA Ops:
  0.0 71.8 %shard_map.100 = f32[2,8,3584]{2,1,0:T(8,128)} custom-call(f32[1536]{0:T(1024)} %gain_ref.1, bf16[8,1536]{1,0:T(8,128)(2,1)} %ql_ref.1, bf16[8,576]{1,0:T(8,128)(2,1)} %nk_ref.1, s32[2]{0:T(128)} %len_ref.1, s32[2]{0:T(128)} %count_ref.1, bf16[1536,768]{1,0:T(8,128)(2,1)} %qup_hbm.1, bf16[4,128,512]{2,1,0:T(8,128)(2,1)} %wuk_hbm.1, ...), custom_call_target="tpu_custom_call" | custom-call | tf_op jit(solution)/shard_map/pallas_call | solution.py:460
  71.8 1.6 %convert_element_type.9 = bf16[2,8,3584]{2,1,0:T(8,128)(2,1)} convert(f32[2,8,3584]{2,1,0:T(8,128)} %shard_map.100) | non-fusion elementwise | flops 57344 | bytes 344064 | tf_op jit(solution)/shard_map/convert_element_type | solution.py:503

commit v5 on v4

--- a/solution.py
+++ b/solution.py
@@ -28,7 +28,7 @@
 
 
 def column_chunks(width):
-    for parts in (4, 3, 2):
+    for parts in (2, 3):
         if width % (parts * 128) == 0:
             return parts
     return 1

time: 73.6 us -> 74 us (level)
  no operation moved by 1% of the time
where the time goes in v5:
time: 74 us; the launch traced here: 73.8 us
  Pallas kernels  72.2 us (98%)
  other arithmetic  1.6 us (2%)
    pallas_call x1, Pallas kernels, mix_call(): pl.pallas_call(functools.partial(mix, (tensors, copies, rows_dev)), out_s...  72.2 us
    convert_element_type x1, other arithmetic, shards(): return placed.astype(jnp.bfloat16)  1.6 us

profile of v5, /device:TPU:0, one launch (start us, length us, event | category | flops | bytes accessed | tf_op | source)
XLA Modules:
  0.0 73.8 jit_solution(2624772103759811577)
XLA Ops:
  0.0 72.2 %shard_map.100 = f32[2,8,3584]{2,1,0:T(8,128)} custom-call(f32[1536]{0:T(1024)} %gain_ref.1, bf16[8,1536]{1,0:T(8,128)(2,1)} %ql_ref.1, bf16[8,576]{1,0:T(8,128)(2,1)} %nk_ref.1, s32[2]{0:T(128)} %len_ref.1, s32[2]{0:T(128)} %count_ref.1, bf16[1536,768]{1,0:T(8,128)(2,1)} %qup_hbm.1, bf16[4,128,512]{2,1,0:T(8,128)(2,1)} %wuk_hbm.1, ...), custom_call_target="tpu_custom_call" | custom-call | tf_op jit(solution)/shard_map/pallas_call | solution.py:460
  72.2 1.6 %convert_element_type.9 = bf16[2,8,3584]{2,1,0:T(8,128)(2,1)} convert(f32[2,8,3584]{2,1,0:T(8,128)} %shard_map.100) | non-fusion elementwise | flops 57344 | bytes 344064 | tf_op jit(solution)/shard_map/convert_element_type | solution.py:503
